TPU v7x, 32 devices: a whole 2x2x4 slice. The times are simulated.
32 devices in a mesh: row: 16 (over z, x, core), col: 2 (over y).
Axes of the slice: x: 2, y: 2, z: 4, core: 2. Of those that a mesh axis runs over, the one named last changes fastest.
Arguments:
- tensor: bfloat16 [1024, 512, 256], P('row', 'col'), may hold values from -8.808155 to 8.808155
- factor_a: float32 [1024, 256], P(('row', 'col')), may hold values from -0.59375 to 0.59375
- factor_b: float32 [512, 256], P(('col', 'row')), may hold values from -0.8396893 to 0.8396893
- factor_c: float32 [256, 256], replicated, may hold values from -1.1875 to 1.1875
Outputs:
- grad_a: float32 [1024, 256], P(('row', 'col'))
- grad_b: float32 [512, 256], P(('col', 'row'))
- grad_c: float32 [256, 256], replicated
All inputs are finite; a program needn't handle non-finite values.
Results may differ from a plain program's by a relative error of at most 0.0018.
Values sent between devices are 32-bit elements; how exact they have to be, the bound alone decides.
A program may use at most 128 MiB of HBM per device.

v0:
```python
import jax
import jax.numpy as jnp
from jax import lax
from jax.sharding import PartitionSpec as P


def self_product(matrix):
    return jnp.dot(matrix.T, matrix, precision=lax.Precision.HIGHEST)


def shards(tensor, factor_a, factor_b, factor_c):
    highest = lax.Precision.HIGHEST
    a_block = lax.all_gather(factor_a, "col", axis=0, tiled=True)
    b_block = lax.all_gather(factor_b, "row", axis=0, tiled=True)
    gram_c = self_product(factor_c)
    gram_a, gram_b = lax.psum((self_product(factor_a), self_product(factor_b)), ("row", "col"))
    c_low = factor_c.astype(jnp.bfloat16)
    contracted = jnp.einsum("ijk,kr->ijr", tensor, c_low, preferred_element_type=jnp.float32)
    mttkrp_a = jnp.einsum("ijr,jr->ir", contracted, b_block, precision=highest)
    mttkrp_b = jnp.einsum("ijr,ir->jr", contracted, a_block, precision=highest)
    rows_a = tensor.shape[0]
    rows_b = tensor.shape[1]
    depth = tensor.shape[2]
    panel = (a_block[:, None, :] * b_block[None, :, :]).astype(jnp.bfloat16)
    panel = panel.reshape(rows_a * rows_b, panel.shape[2])
    flat = tensor.reshape(rows_a * rows_b, depth)
    mttkrp_c = lax.dot_general(
        flat, panel, (((0,), (0,)), ((), ())), preferred_element_type=jnp.float32
    )
    total_c = lax.psum(mttkrp_c, ("row", "col"))
    owned_a = lax.psum_scatter(mttkrp_a, "col", scatter_dimension=0, tiled=True)
    owned_b = lax.psum_scatter(mttkrp_b, "row", scatter_dimension=0, tiled=True)
    grad_a = jnp.dot(factor_a, gram_b * gram_c, precision=highest) - owned_a
    grad_b = jnp.dot(factor_b, gram_a * gram_c, precision=highest) - owned_b
    grad_c = jnp.dot(factor_c, gram_a * gram_b, precision=highest) - total_c
    return (grad_a, grad_b, grad_c)


def solution(mesh):
    in_specs = (P("row", "col", None), P(("row", "col"), None), P(("col", "row"), None), P())
    out_specs = (P(("row", "col"), None), P(("col", "row"), None), P())
    return jax.shard_map(shards, mesh=mesh, in_specs=in_specs, out_specs=out_specs, check_vma=False)
```

profile of v0, /device:TPU:1, one launch (start us, length us, event | category | flops | bytes accessed | tf_op | source)
XLA Modules:
  0.0 189.2 jit_solution(8704696142767923138)
XLA Ops:
  8.0 0.0 copy-start
  8.0 0.0 all-reduce.3.cloned.1.call-start
  8.1 24.0 %all_gather.6 = f32[256,256]{1,0:T(8,128)S(1)} all-gather(f32[16,256]{1,0:T(8,128)} %param.6), channel_id=1, replica_groups=mesh['row'=16,'col'=2] {'row'}, dimensions={0}, use_global_device_ids=true | all-gather | bytes 278528 | tf_op jit(solution)/shard_map/all_gather | solution.py:14
  32.1 1.9 %fusion.13 = f32[256,256]{1,0:T(8,128)} fusion(f32[16,256]{1,0:T(8,128)} %param.6), kind=kOutput, calls=%fused_computation.19 | convolution fusion | flops 12582912 | bytes 278528 | tf_op jit(solution)/shard_map/dot_general | solution.py:8
  34.0 3.6 %all_gather.7 = f32[64,256]{1,0:T(8,128)S(1)} all-gather(f32[32,256]{1,0:T(8,128)} %param.5), channel_id=1, replica_groups=mesh['row'=16,'col'=2] {'col'}, dimensions={0}, use_global_device_ids=true | all-gather | bytes 98304 | tf_op jit(solution)/shard_map/all_gather | solution.py:13
  37.7 2.0 %fusion.15 = f32[256,256]{1,0:T(8,128)} fusion(f32[32,256]{1,0:T(8,128)} %param.5), kind=kOutput, calls=%fused_computation.21 | convolution fusion | flops 25165824 | bytes 294912 | tf_op jit(solution)/shard_map/dot_general | solution.py:8
  39.6 0.1 copy.7
  39.7 8.4 %fusion.4 = f32[256,256]{0,1:T(8,128)} fusion(bf16[64,256,256]{2,1,0:T(8,128)(2,1)} %param.4, f32[256,256]{0,1:T(8,128)S(1)} %copy.7, f32[64,256]{1,0:T(8,128)S(1)} %all_gather.7), kind=kOutput, calls=%fused_computation.8 | convolution fusion | flops 2155872256 | bytes 8978432 | tf_op jit(solution)/shard_map/dot_general | solution.py:27
  48.1 0.0 all-reduce.3.cloned.1.call-update
  48.1 0.0 reduce-scatter.5.cloned.1.call-start
  48.2 0.0 copy-done
  48.2 12.1 %multiply_reduce_fusion.1 = (f32[256,64]{0,1:T(8,128)}, f32[64,256,256]{2,1,0:T(8,128)}) fusion(f32[256,256]{0,1:T(8,128)S(1)} %bitcast.40, bf16[64,256,256]{2,1,0:T(8,128)(2,1)} %param.4, f32[256,256]{1,0:T(8,128)S(1)} %copy-done), kind=kOutput, calls=%fused_computation.1 | convolution fusion | flops 2155921408 | bytes 25755648 | tf_op jit(solution)/shard_map/ijk,kr->ijr/dot_general | solution.py:18
  60.3 0.0 copy-start.2
  60.3 0.0 copy-start.1
  60.3 8.5 %multiply_reduce_fusion = f32[256,256]{0,1:T(8,128)} fusion(f32[64,256,256]{2,1,0:T(8,128)} %get-tuple-element.10, f32[256,64]{0,1:T(8,128)S(1)} %bitcast.43), kind=kLoop, calls=%fused_computation | loop fusion | flops 8323072 | bytes 17104896 | tf_op jit(solution)/shard_map/ijr,ir->jr/dot_general | solution.py:20
  68.7 0.0 reduce-scatter.5.cloned.1.call-update
  68.8 0.0 reduce-scatter.3.cloned.1.call-start
  68.8 0.5 reduce-scatter.3.cloned.1.call-update
  69.4 0.6 fusion.14
  70.0 105.6 %all-reduce.3.cloned.1.call-done = (f32[256,256]{1,0:T(8,128)}, f32[256,256]{1,0:T(8,128)}, f32[256,256]{0,1:T(8,128)}) async-done(((f32[256,256]{1,0:T(8,128)}, f32[256,256]{1,0:T(8,128)}, f32[256,256]{0,1:T(8,128)}), (f32[256,256]{1,0:T(8,128)}, f32[256,256]{1,0:T(8,128)}, f32[256,256]{0,1:T(8,128)})) %all-reduce.3.cloned.1.call-update) | async-done | bytes 786448 | tf_op jit(solution)/shard_map/psum | solution.py:16
  175.5 1.7 fusion.3
  177.2 0.8 copy.8
  178.1 0.0 reduce-scatter.5.cloned.1.call-done
  178.1 0.0 copy-done.2
  178.1 1.8 fusion.6
  179.9 0.0 reduce-scatter.3.cloned.1.call-done
  179.9 0.0 copy-done.1
  179.9 1.8 fusion.5
Async XLA Ops:
  8.0 40.2 %copy-start = (f32[256,256]{1,0:T(8,128)S(1)}, f32[256,256]{1,0:T(8,128)}, u32[]{:S(2)}) copy-start(f32[256,256]{1,0:T(8,128)} %param.7) | copy-start | bytes 786436
  8.0 167.5 %all-reduce.3.cloned.1.call-start = ((), (), s32[]{:S(2)}) async-start(), calls=%async_computation.4 | async-start | bytes 1572864 | tf_op jit(solution)/shard_map/psum | solution.py:16
  48.1 130.0 %reduce-scatter.5.cloned.1.call-start = ((), (), s32[]{:S(2)}) async-start(), calls=%async_computation.3 | async-start | bytes 278528 | tf_op jit(solution)/shard_map/reduce_scatter | solution.py:32
  60.3 117.8 %copy-start.2 = (f32[16,256]{1,0:T(8,128)S(1)}, f32[16,256]{1,0:T(8,128)}, u32[]{:S(2)}) copy-start(f32[16,256]{1,0:T(8,128)} %param.6) | copy-start | bytes 49156
  60.3 119.6 %copy-start.1 = (f32[32,256]{1,0:T(8,128)S(1)}, f32[32,256]{1,0:T(8,128)}, u32[]{:S(2)}) copy-start(f32[32,256]{1,0:T(8,128)} %param.5) | copy-start | bytes 98308
  68.8 111.1 %reduce-scatter.3.cloned.1.call-start = ((), (), s32[]{:S(2)}) async-start(), calls=%async_computation.2 | async-start | bytes 98304 | tf_op jit(solution)/shard_map/reduce_scatter | solution.py:31
Sparse Core Ops, SparseCore 0:
  48.2 127.2 all-reduce.2
Sparse Core Ops, SparseCore 1:
  68.8 51.4 reduce-scatter.4
  122.3 10.2 reduce-scatter.2
where the time goes:
time: 191 us; the launch traced here: 189 us
  waiting for transfers between devices  106 us (55%)
  matrix products  30.2 us (16%)
  blocking collectives  27.7 us (15%)
  between operations  15.5 us (8%)
  other arithmetic  8.47 us (4%)
    psum x1, waiting for transfers between devices, shards(): lax.psum((self_product(factor_a), self_product(factor_b)), ('row', 'col'))  106 us
    all_gather x1, blocking collectives, shards(): b_block = lax.all_gather(factor_b, 'row', axis=0, tiled=True)  24 us
    dot_general x1, matrix products, shards(): jnp.einsum('ijk,kr->ijr', tensor, c_low, preferred_element_type=jnp.float32)  12.1 us
    dot_general x1, other arithmetic, shards(): mttkrp_b = jnp.einsum('ijr,ir->jr', contracted, a_block, precision=highest)  8.47 us
    dot_general x1, matrix products, shards(): lax.dot_general(flat, panel, (((0,), (0,)), ((), ())), preferred_element_...  8.36 us
    dot_general x3, matrix products, self_product(): return jnp.dot(matrix.T, matrix, precision=lax.Precision.HIGHEST)  4.46 us
  transfers between devices with their start and end apart: 3, of which 1 were waited for; matrix products, arithmetic and copies ran while one was open for 13% of the time, Pallas kernels for 0%

commit v1 on v0

v1 whole, which is shorter than its diff:
```python
import functools

import jax
import jax.numpy as jnp
from jax import lax
from jax.experimental import pallas as pl
from jax.experimental.pallas import tpu as pltpu
from jax.sharding import PartitionSpec as P

MESH = pl.DeviceIdType.MESH
HIGHEST = lax.Precision.HIGHEST
GROUP = 4


def dot(left, right):
    return jnp.dot(left, right, precision=HIGHEST, preferred_element_type=jnp.float32)


def kernel(
    n_row, n_col,
    t_hbm, fa_ref, fb_ref, fc_ref,
    out_a, out_b, out_c,
    t_ref, x_ref, a_gather, b_gather, a_ref, c_low, gram_c,
    part_ga, part_mb, part_mc, mate_ga, mate_mb, mate_mc, half_ga, half_mb, half_mc,
    peer_ga, peer_mb, peer_mc, col_ma, col_gb, col_mc, part_gb, part_ma,
    grams, final_c,
    load_sem, row_send, row_recv, mate_send, mate_recv, col_send, col_recv,
):
    row, col = lax.axis_index("row"), lax.axis_index("col")
    chips = n_row // 2
    chip, core = row // 2, lax.rem(row, 2)
    mate = {"row": row + 1 - 2 * core}
    rows_i, rows_j, depth = t_ref.shape
    rank = fa_ref.shape[1]
    own_a, own_b = fa_ref.shape[0], fb_ref.shape[0]
    steps = rows_i // GROUP
    sends = []

    def at_chip(shift):
        return lax.rem(chip + shift, chips)

    def across_row(phase, source, target):
        def copies():
            for shift in range(1, chips):
                other = at_chip(shift)
                yield pltpu.make_async_remote_copy(
                    src_ref=source(other), dst_ref=target,
                    send_sem=row_send.at[phase, shift], recv_sem=row_recv.at[phase, shift],
                    device_id={"row": 2 * other + core}, device_id_type=MESH,
                )
        made = list(copies())
        for copy in made:
            copy.start()
        sends.extend(made)
        return made

    def across_mate(phase, source, target):
        copy = pltpu.make_async_remote_copy(
            src_ref=source, dst_ref=target,
            send_sem=mate_send.at[phase], recv_sem=mate_recv.at[phase],
            device_id=mate, device_id_type=MESH,
        )
        copy.start()
        sends.append(copy)
        return [copy]

    def across_col(phase, source, target):
        made = []
        for shift in range(1, n_col):
            other = lax.rem(col + shift, n_col)
            copy = pltpu.make_async_remote_copy(
                src_ref=source(other), dst_ref=target,
                send_sem=col_send.at[phase, shift], recv_sem=col_recv.at[phase, shift],
                device_id={"col": other}, device_id_type=MESH,
            )
            copy.start()
            made.append(copy)
        sends.extend(made)
        return made

    def arrive(made):
        for copy in made:
            copy.wait_recv()

    def load(step):
        part = pl.ds(step * GROUP, GROUP)
        return pltpu.make_async_copy(t_hbm.at[part], t_ref.at[part], load_sem.at[step])

    for step in range(steps):
        load(step).start()

    barrier = pltpu.get_barrier_semaphore()
    pl.semaphore_signal(barrier, inc=1, device_id=mate, device_id_type=MESH)
    for shift in range(1, chips):
        pl.semaphore_signal(
            barrier, inc=1, device_id={"row": 2 * at_chip(shift) + core}, device_id_type=MESH
        )
    for shift in range(1, n_col):
        pl.semaphore_signal(
            barrier, inc=1, device_id={"col": lax.rem(col + shift, n_col)}, device_id_type=MESH
        )
    a_gather[col] = fa_ref[...]
    b_gather[chip, core] = fb_ref[...]
    pl.semaphore_wait(barrier, chips + n_col - 1)

    a_moves = across_col(0, lambda other: a_gather.at[col], a_gather.at[col])
    b_moves = across_row(0, lambda other: b_gather.at[chip, core], b_gather.at[chip, core])
    factor_c = fc_ref[...]
    c_low[...] = factor_c.astype(jnp.bfloat16)
    gram_c[...] = dot(factor_c.T, factor_c)
    part_mb[...] = jnp.zeros_like(part_mb)
    part_mc[...] = jnp.zeros_like(part_mc)
    arrive(a_moves)
    a_block = a_gather[...].reshape(rows_i, rank)
    a_ref[...] = a_block
    part_ga[...] = dot(a_block.T, a_block).reshape(part_ga.shape)
    ga_mate = across_mate(0, part_ga.at[:, 1 - core], mate_ga)

    def first_pass(begin, end):
        @pl.loop(begin, end)
        def _(step):
            load(step).wait()
            base = step * GROUP
            flat = t_ref[pl.ds(base, GROUP)].reshape(GROUP * rows_j, depth)
            product = jnp.dot(flat, c_low[...], preferred_element_type=jnp.float32)
            product = product.reshape(GROUP, rows_j, rank)
            x_ref[pl.ds(base, GROUP)] = product
            total = part_mb[...].reshape(rows_j, rank)
            for i in range(GROUP):
                total += product[i] * a_ref[pl.ds(base + i, 1), :]
            part_mb[...] = total.reshape(part_mb.shape)

    def second_pass(begin, end):
        @pl.loop(begin, end)
        def _(step):
            base = step * GROUP
            b_block = b_gather[...].reshape(rows_j, rank)
            panels = []
            for i in range(GROUP):
                a_row = a_ref[pl.ds(base + i, 1), :]
                panels.append((a_row * b_block).astype(jnp.bfloat16))
                part_ma[pl.ds(base + i, 1), :] = jnp.sum(
                    x_ref[base + i] * b_block, axis=0, keepdims=True
                )
            panel = jnp.concatenate(panels, axis=0)
            flat = t_ref[pl.ds(base, GROUP)].reshape(GROUP * rows_j, depth)
            product = lax.dot_general(
                flat, panel, (((0,), (0,)), ((), ())), preferred_element_type=jnp.float32
            )
            part_mc[...] += product.reshape(part_mc.shape)

    first_pass(0, steps // 2)
    arrive(ga_mate)
    half_ga[...] = part_ga[:, core] + mate_ga[...]
    ga_moves = across_row(1, lambda other: half_ga.at[other], peer_ga.at[chip])
    peer_ga[chip] = half_ga[chip]
    arrive(b_moves)
    b_mate = across_mate(1, b_gather.at[:, core], b_gather.at[:, core])
    first_pass(steps // 2, steps)
    mb_mate = across_mate(2, part_mb.at[:, 1 - core], mate_mb)
    arrive(b_mate)
    b_block = b_gather[...].reshape(rows_j, rank)
    part_gb[...] = dot(b_block.T, b_block).reshape(part_gb.shape)
    col_gb[col] = part_gb[row]
    gb_moves = across_col(1, lambda other: part_gb.at[row], col_gb.at[col])
    second_pass(0, steps // 4)
    arrive(mb_mate)
    half_mb[...] = part_mb[:, core] + mate_mb[...]
    mb_moves = across_row(2, lambda other: half_mb.at[other], peer_mb.at[chip])
    peer_mb[chip] = half_mb[chip]
    arrive(ga_moves)
    arrive(gb_moves)
    gram_rows = [jnp.sum(peer_ga[...], axis=0), jnp.sum(col_gb[...], axis=0)]
    grams[chip, core] = jnp.stack(gram_rows)
    gram_moves = across_row(3, lambda other: grams.at[chip, core], grams.at[chip, core])
    second_pass(steps // 4, steps)

    mc_mate = across_mate(3, part_mc.at[:, 1 - core], mate_mc)
    ma_moves = across_col(
        2,
        lambda other: part_ma.at[pl.ds(pl.multiple_of(other * own_a, 8), own_a)],
        col_ma.at[col],
    )
    col_ma[col] = part_ma[pl.ds(pl.multiple_of(col * own_a, 8), own_a), :]
    arrive(gram_moves)
    gram_mate = across_mate(4, grams.at[:, core], grams.at[:, core])
    arrive(mc_mate)
    half_mc[...] = part_mc[:, core] + mate_mc[...]
    mc_moves = across_row(4, lambda other: half_mc.at[other], peer_mc.at[chip])
    peer_mc[chip] = half_mc[chip]
    arrive(gram_mate)
    gram_a = grams[:, :, 0].reshape(rank, rank)
    gram_b = grams[:, :, 1].reshape(rank, rank)
    slice_c = depth // n_row
    rows_c = fc_ref[pl.ds(pl.multiple_of(row * slice_c, 8), slice_c), :]
    model_c = dot(rows_c, gram_a * gram_b)
    arrive(mc_moves)
    total_c = jnp.sum(peer_mc[...], axis=0)
    col_mc[col] = total_c
    c_moves = across_col(3, lambda other: col_mc.at[col], col_mc.at[col])
    model_a = dot(fa_ref[...], gram_b * gram_c[...])
    model_b = dot(fb_ref[...], gram_a * gram_c[...])
    arrive(c_moves)
    final_c[chip, core] = model_c - jnp.sum(col_mc[...], axis=0)
    final_moves = across_row(5, lambda other: final_c.at[chip, core], final_c.at[chip, core])
    arrive(ma_moves)
    out_a[...] = model_a - jnp.sum(col_ma[...], axis=0)
    arrive(mb_moves)
    out_b[...] = model_b - jnp.sum(peer_mb[...], axis=0)
    arrive(final_moves)
    final_mate = across_mate(5, final_c.at[:, core], final_c.at[:, core])
    arrive(final_mate)
    out_c[...] = final_c[...]
    for copy in sends:
        copy.wait_send()


def shards(n_row, n_col, tensor, factor_a, factor_b, factor_c):
    rows_i, rows_j, depth = tensor.shape
    own_a, rank = factor_a.shape
    own_b = factor_b.shape[0]
    chips = n_row // 2
    part_r, part_k = rank // n_row, depth // n_row
    f32 = jnp.float32

    def buffer(*shape):
        return pltpu.VMEM(shape + (rank,), f32)

    vmem = pl.BlockSpec(memory_space=pltpu.VMEM)
    grad_a, grad_b, grad_c = pl.pallas_call(
        functools.partial(kernel, n_row, n_col),
        out_shape=(
            jax.ShapeDtypeStruct((own_a, rank), f32),
            jax.ShapeDtypeStruct((own_b, rank), f32),
            jax.ShapeDtypeStruct((chips, 2, part_k, rank), f32),
        ),
        in_specs=[pl.BlockSpec(memory_space=pl.ANY), vmem, vmem, vmem],
        out_specs=(vmem, vmem, vmem),
        scratch_shapes=[
            pltpu.VMEM(tensor.shape, tensor.dtype),
            buffer(rows_i, rows_j),
            buffer(n_col, own_a),
            buffer(chips, 2, own_b),
            buffer(rows_i),
            pltpu.VMEM((depth, rank), jnp.bfloat16),
            buffer(rank),
            buffer(chips, 2, part_r), buffer(chips, 2, own_b), buffer(chips, 2, part_k),
            buffer(chips, part_r), buffer(chips, own_b), buffer(chips, part_k),
            buffer(chips, part_r), buffer(chips, own_b), buffer(chips, part_k),
            buffer(chips, part_r), buffer(chips, own_b), buffer(chips, part_k),
            buffer(n_col, own_a),
            buffer(n_col, part_r),
            buffer(n_col, part_k),
            buffer(n_row, part_r),
            buffer(rows_i),
            buffer(chips, 2, 2, part_r),
            buffer(chips, 2, part_k),
            pltpu.SemaphoreType.DMA((rows_i // GROUP,)),
            pltpu.SemaphoreType.DMA((6, chips)),
            pltpu.SemaphoreType.DMA((6, chips)),
            pltpu.SemaphoreType.DMA((6,)),
            pltpu.SemaphoreType.DMA((6,)),
            pltpu.SemaphoreType.DMA((4, n_col)),
            pltpu.SemaphoreType.DMA((4, n_col)),
        ],
        compiler_params=pltpu.CompilerParams(
            collective_id=0, has_side_effects=True, vmem_limit_bytes=52 * 1024 * 1024
        ),
        cost_estimate=pl.CostEstimate(
            flops=4 * rows_i * rows_j * depth * rank,
            bytes_accessed=2 * rows_i * rows_j * depth,
            transcendentals=0,
        ),
    )(tensor, factor_a, factor_b, factor_c)
    return grad_a, grad_b, grad_c.reshape(depth, rank)


def solution(mesh):
    in_specs = (P("row", "col", None), P(("row", "col"), None), P(("col", "row"), None), P())
    out_specs = (P(("row", "col"), None), P(("col", "row"), None), P())
    body = functools.partial(shards, mesh.shape["row"], mesh.shape["col"])
    return jax.shard_map(body, mesh=mesh, in_specs=in_specs, out_specs=out_specs, check_vma=False)
```

time: 191 us -> 44.6 us (0.23)
  waiting for transfers between devices: 106 us -> 0 us
  Pallas kernels: 0 us -> 39.4 us
  matrix products: 30.2 us -> 0 us
  blocking collectives: 27.7 us -> 0 us
  between operations: 15.5 us -> 0.65 us
  other arithmetic: 8.47 us -> 0 us
  local copies, waits for them, and re-layouts: 0.98 us -> 4.34 us
    psum x1 -> x0, waiting for transfers between devices: 106 us -> none  [shards(): lax.psum((self_product(factor_a), self_product(factor_b)), ('row', 'col'))]
    pallas_call x0 -> x1, Pallas kernels: none -> 39.4 us  [shards(): pl.pallas_call(functools.partial(kernel, n_row, n_col), out_shape=(jax.Sh...]
    dot_general x8 -> x0, matrix products: 30.2 us -> none  [the longest x1 12.1 us: shards(): jnp.einsum('ijk,kr->ijr', tensor, c_low, preferred_element_type=jnp.float32)]
    all_gather x2 -> x0, blocking collectives: 27.7 us -> none  [the longest x1 24 us: shards(): b_block = lax.all_gather(factor_b, 'row', axis=0, tiled=True)]
    dot_general x1 -> x0, other arithmetic: 8.47 us -> none  [shards(): mttkrp_b = jnp.einsum('ijr,ir->jr', contracted, a_block, precision=highest)]
    unnamed x7 -> x9, local copies, waits for them, and re-layouts: 0.85 us -> 4.34 us
  transfers between devices with their start and end apart: 3 -> 0, of which waited for: 1 -> 0; matrix products, arithmetic and copies ran while one was open for 13% -> 0% of each run, Pallas kernels for 0% -> 0%
where the time goes in v1:
time: 44.6 us; the launch traced here: 44.3 us
  Pallas kernels  39.4 us (88%)
  local copies, waits for them, and re-layouts  4.34 us (10%)
  between operations  0.65 us (1%)
    pallas_call x1, Pallas kernels, shards(): pl.pallas_call(functools.partial(kernel, n_row, n_col), out_shape=(jax.Sh...  39.4 us
    unnamed x9, local copies, waits for them, and re-layouts  4.34 us

profile of v1, /device:TPU:1, one launch (start us, length us, event | category | flops | bytes accessed | tf_op | source)
XLA Modules:
  0.0 44.3 jit_solution(10666622593045999624)
XLA Ops:
  0.6 0.0 copy-start
  0.6 0.9 %copy-done = f32[256,256]{1,0:T(8,128)S(1)} copy-done((f32[256,256]{1,0:T(8,128)S(1)}, f32[256,256]{1,0:T(8,128)}, u32[]{:S(2)}) %copy-start) | copy-done | bytes 262168
  1.6 0.0 copy-start.1
  1.6 0.8 %copy-done.1 = f32[32,256]{1,0:T(8,128)S(1)} copy-done((f32[32,256]{1,0:T(8,128)S(1)}, f32[32,256]{1,0:T(8,128)}, u32[]{:S(2)}) %copy-start.1) | copy-done | bytes 32792
  2.3 0.0 copy-start.2
  2.3 0.7 %copy-done.2 = f32[16,256]{1,0:T(8,128)S(1)} copy-done((f32[16,256]{1,0:T(8,128)S(1)}, f32[16,256]{1,0:T(8,128)}, u32[]{:S(2)}) %copy-start.2) | copy-done | bytes 16408
  3.1 39.4 %shard_map.67 = (f32[32,256]{1,0:T(8,128)S(1)}, f32[16,256]{1,0:T(8,128)S(1)}, f32[8,2,16,256]{3,2,1,0:T(8,128)S(1)}) custom-call(bf16[64,256,256]{2,1,0:T(8,128)(2,1)} %t_hbm.1, f32[32,256]{1,0:T(8,128)S(1)} %copy-done.1, f32[16,256]{1,0:T(8,128)S(1)} %copy-done.2, f32[256,256]{1,0:T(8,128)S(1)} %copy-done), custom_call_target="tpu_custom_call" | custom-call | flops 4294967296 | bytes 8388608 | tf_op jit(solution)/shard_map/pallas_call | solution.py:230
  42.4 0.6 %copy.10 = f32[32,256]{1,0:T(8,128)} copy(f32[32,256]{1,0:T(8,128)S(1)} %get-tuple-element.12) | data formatting | bytes 65536
  43.0 0.6 %copy.11 = f32[16,256]{1,0:T(8,128)} copy(f32[16,256]{1,0:T(8,128)S(1)} %get-tuple-element.13) | data formatting | bytes 32768
  43.6 0.7 %copy.12 = f32[256,256]{1,0:T(8,128)} copy(f32[256,256]{1,0:T(8,128)S(1)} %bitcast.1) | data formatting | bytes 524288
Async XLA Ops:
  0.6 1.0 %copy-start = (f32[256,256]{1,0:T(8,128)S(1)}, f32[256,256]{1,0:T(8,128)}, u32[]{:S(2)}) copy-start(f32[256,256]{1,0:T(8,128)} %fc_ref.1) | copy-start | bytes 786436
  1.6 0.8 %copy-start.1 = (f32[32,256]{1,0:T(8,128)S(1)}, f32[32,256]{1,0:T(8,128)}, u32[]{:S(2)}) copy-start(f32[32,256]{1,0:T(8,128)} %fa_ref.1) | copy-start | bytes 98308
  2.3 0.7 %copy-start.2 = (f32[16,256]{1,0:T(8,128)S(1)}, f32[16,256]{1,0:T(8,128)}, u32[]{:S(2)}) copy-start(f32[16,256]{1,0:T(8,128)} %fb_ref.1) | copy-start | bytes 49156

commit v2 on v1

v2 whole, which is shorter than its diff:
```python
import functools

import jax
import jax.numpy as jnp
from jax import lax
from jax.experimental import pallas as pl
from jax.experimental.pallas import tpu as pltpu
from jax.sharding import PartitionSpec as P

MESH = pl.DeviceIdType.MESH
HIGHEST = lax.Precision.HIGHEST
GROUP = 8
WIDE = 32
BLOCKS = 5


def dot(left, right):
    return jnp.dot(left, right, precision=HIGHEST, preferred_element_type=jnp.float32)


def kernel(
    n_row, n_col, parts,
    t_hbm, fa_hbm, fb_hbm, fc_hbm,
    out_a, out_b, out_c,
    t_ref, x_ref, a_gather, b_gather, a_ref, fc_ref, c_low, gram_c,
    part_ga, part_mb, part_mc, mate_ga, mate_mb, mate_mc, half_ga, half_mb, half_mc,
    peer_ga, peer_mb, peer_mc, col_ma, col_gb, part_gb, part_ma, sums_ma,
    grams, final_c,
    load_sem, in_sem, row_send, row_recv, c_send, c_recv, mate_send, mate_recv, col_send, col_recv,
):
    row, col = lax.axis_index("row"), lax.axis_index("col")
    chips = n_row // 2
    chip, core = row // 2, lax.rem(row, 2)
    mate = {"row": row + 1 - 2 * core}
    rows_i, rows_j, depth = t_ref.shape
    rank = a_ref.shape[1]
    own_a, own_b = fa_hbm.shape[0], fb_hbm.shape[0]
    steps = rows_i // GROUP
    sends = []

    def chip_at(flip):
        other, bit = chip, 1
        while bit < chips:
            if flip & bit:
                other += bit * (1 - 2 * lax.rem(chip // bit, 2))
            bit *= 2
        return other

    def place(flip, shift):
        return chip_at(flip), lax.rem(col + shift, n_col)

    everyone = [(f, s) for f in range(chips) for s in range(n_col) if f or s]

    def send(source, target, send_sem, recv_sem, device):
        copy = pltpu.make_async_remote_copy(
            src_ref=source, dst_ref=target, send_sem=send_sem, recv_sem=recv_sem,
            device_id=device, device_id_type=MESH,
        )
        copy.start()
        sends.append(copy)
        return copy

    def across_row(phase, source, target):
        return [
            send(
                source(chip_at(flip)), target, row_send.at[phase, flip], row_recv.at[phase, flip],
                {"row": 2 * chip_at(flip) + core},
            )
            for flip in range(1, chips)
        ]

    def across_mate(phase, source, target):
        return send(source, target, mate_send.at[phase], mate_recv.at[phase], mate)

    def across_col(phase, source, target):
        return [
            send(
                source(place(0, shift)[1]), target,
                col_send.at[phase, shift], col_recv.at[phase, shift],
                {"col": place(0, shift)[1]},
            )
            for shift in range(1, n_col)
        ]

    def across_all(phase, reach, source, target):
        made = []
        for flip, shift in reach:
            other, other_col = place(flip, shift)
            made.append(send(
                source(other, other_col), target,
                c_send.at[phase, flip, shift], c_recv.at[phase, flip, shift],
                {"row": 2 * other + core, "col": other_col},
            ))
        return made

    def arrive(made):
        for copy in made:
            copy.wait_recv()

    def load(step):
        part = pl.ds(step * GROUP, GROUP)
        return pltpu.make_async_copy(t_hbm.at[part], t_ref.at[part], load_sem.at[step])

    barrier = pltpu.get_barrier_semaphore()
    pl.semaphore_signal(barrier, inc=1, device_id=mate, device_id_type=MESH)
    for flip, shift in everyone:
        other, other_col = place(flip, shift)
        pl.semaphore_signal(
            barrier, inc=1, device_id={"row": 2 * other + core, "col": other_col},
            device_id_type=MESH,
        )
    fc_load = pltpu.make_async_copy(fc_hbm, fc_ref, in_sem.at[0])
    fb_load = pltpu.make_async_copy(fb_hbm, b_gather.at[chip, core], in_sem.at[1])
    fa_load = pltpu.make_async_copy(fa_hbm, a_gather.at[col], in_sem.at[2])
    fc_load.start()
    fb_load.start()
    fa_load.start()
    for step in range(steps):
        load(step).start()

    def contract(begin, end):
        @pl.loop(begin, end)
        def _(step):
            load(step).wait()
            base = step * GROUP
            flat = t_ref[pl.ds(base, GROUP)].reshape(GROUP * rows_j, depth)
            product = jnp.dot(flat, c_low[...], preferred_element_type=jnp.float32)
            x_ref[pl.ds(base, GROUP)] = product.reshape(GROUP, rows_j, rank)

    def sum_over_i():
        @pl.loop(0, steps)
        def _(step):
            base = step * GROUP
            total = part_mb[...].reshape(rows_j, rank)
            for i in range(GROUP):
                total += x_ref[base + i] * a_ref[pl.ds(base + i, 1), :]
            part_mb[...] = total.reshape(part_mb.shape)

    width = 2 * own_b

    def use_block(other):
        begin = pl.multiple_of(other * width, width)
        b_part = b_gather[other].reshape(width, rank)

        @pl.loop(0, rows_i // WIDE)
        def _(step):
            base = step * WIDE
            panels = []
            for i in range(WIDE):
                a_row = a_ref[pl.ds(base + i, 1), :]
                panels.append((a_row * b_part).astype(jnp.bfloat16))
                terms = x_ref[base + i, pl.ds(begin, width), :] * b_part
                sums_ma[base + i] += jnp.sum(terms.reshape(width // 8, 8, rank), axis=0)
            panel = jnp.concatenate(panels, axis=0)
            flat = t_ref[pl.ds(base, WIDE), pl.ds(begin, width), :].reshape(WIDE * width, depth)
            product = lax.dot_general(
                flat, panel, (((0,), (0,)), ((), ())), preferred_element_type=jnp.float32
            )
            part_mc[...] += product.reshape(part_mc.shape)

    part_mb[...] = jnp.zeros_like(part_mb)
    part_mc[...] = jnp.zeros_like(part_mc)
    sums_ma[...] = jnp.zeros_like(sums_ma)
    fc_load.wait()
    factor_c = fc_ref[...]
    c_low[...] = factor_c.astype(jnp.bfloat16)
    gram_c[...] = dot(factor_c.T, factor_c)
    contract(0, steps // 2)
    fb_load.wait()
    fa_load.wait()
    pl.semaphore_wait(barrier, chips * n_col)

    b_moves = across_row(0, lambda other: b_gather.at[chip, core], b_gather.at[chip, core])
    b_mates = [across_mate(BLOCKS, b_gather.at[chip, core], b_gather.at[chip, core])]
    a_moves = across_col(0, lambda other: a_gather.at[col], a_gather.at[col])
    contract(steps // 2, steps)
    arrive(a_moves)
    a_block = a_gather[...].reshape(rows_i, rank)
    a_ref[...] = a_block
    part_ga[...] = dot(a_block.T, a_block).reshape(part_ga.shape)
    ga_mate = across_mate(0, part_ga.at[:, 1 - core], mate_ga)
    sum_over_i()
    mb_mate = across_mate(1, part_mb.at[:, 1 - core], mate_mb)
    arrive([ga_mate])
    half_ga[...] = part_ga[:, core] + mate_ga[...]
    ga_moves = across_row(1, lambda other: half_ga.at[other], peer_ga.at[chip])
    peer_ga[chip] = half_ga[chip]

    for flip in range(chips):
        if flip + 1 < chips:
            arrive([b_moves[flip]])
            view = b_gather.at[chip_at(flip + 1), core]
            b_mates.append(across_mate(BLOCKS + flip + 1, view, view))
        if flip == chips // 2:
            arrive([mb_mate])
            half_mb[...] = part_mb[:, core] + mate_mb[...]
            mb_moves = across_row(2, lambda other: half_mb.at[other], peer_mb.at[chip])
            peer_mb[chip] = half_mb[chip]
        arrive([b_mates[flip]])
        use_block(chip_at(flip))

    mc_mate = across_mate(2, part_mc.at[:, 1 - core], mate_mc)
    b_block = b_gather[...].reshape(rows_j, rank)
    part_gb[...] = dot(b_block.T, b_block).reshape(part_gb.shape)
    col_gb[col] = part_gb[row]
    gb_moves = across_col(1, lambda other: part_gb.at[row], col_gb.at[col])
    arrive([mc_mate])
    half_mc[...] = part_mc[:, core] + mate_mc[...]
    split = parts == n_col
    mc_moves = across_all(
        0, everyone,
        lambda other, other_col: half_mc.at[other, other_col if split else 0],
        peer_mc.at[chip, col],
    )
    mine = col if split else 0
    peer_mc[chip, col] = half_mc[chip, mine]
    part_ma[...] = jnp.sum(sums_ma[...], axis=1)
    ma_moves = across_col(
        2,
        lambda other: part_ma.at[pl.ds(pl.multiple_of(other * own_a, 8), own_a)],
        col_ma.at[col],
    )
    col_ma[col] = part_ma[pl.ds(pl.multiple_of(col * own_a, 8), own_a), :]
    arrive(ga_moves)
    arrive(gb_moves)
    gram_rows = [jnp.sum(peer_ga[...], axis=0), jnp.sum(col_gb[...], axis=0)]
    grams[chip, core] = jnp.stack(gram_rows)
    gram_moves = across_row(3, lambda other: grams.at[chip, core], grams.at[chip, core])
    arrive(mc_moves)
    pieces = peer_mc[...].reshape((chips * n_col,) + peer_mc.shape[2:])
    final_c[chip, core, mine] = jnp.sum(pieces, axis=0)
    reach = [(f, s) for f, s in everyone if split or s == 0]
    view = final_c.at[chip, core, mine]
    final_moves = across_all(1, reach, lambda other, other_col: view, view)
    arrive(mb_moves)
    arrive(ma_moves)
    arrive(gram_moves)
    gram_mate = across_mate(3, grams.at[:, core], grams.at[:, core])
    arrive([gram_mate])
    gram_a = grams[:, :, 0].reshape(rank, rank)
    gram_b = grams[:, :, 1].reshape(rank, rank)
    own_rows_a = a_gather[col]
    own_rows_b = b_gather[chip, core]
    out_a[...] = dot(own_rows_a, gram_b * gram_c[...]) - jnp.sum(col_ma[...], axis=0)
    out_b[...] = dot(own_rows_b, gram_a * gram_c[...]) - jnp.sum(peer_mb[...], axis=0)
    out_c[...] = dot(fc_ref[...], gram_a * gram_b).reshape(out_c.shape)
    arrive(final_moves)
    final_mate = across_mate(4, final_c.at[:, core], final_c.at[:, core])
    out_c[:, core] -= final_c[:, core]
    arrive([final_mate])
    out_c[:, 1 - core] -= final_c[:, 1 - core]
    for copy in sends:
        copy.wait_send()


def shards(n_row, n_col, tensor, factor_a, factor_b, factor_c):
    rows_i, rows_j, depth = tensor.shape
    own_a, rank = factor_a.shape
    own_b = factor_b.shape[0]
    chips = n_row // 2
    parts = n_col if depth % (8 * n_row * n_col) == 0 else 1
    part_r, part_k = rank // n_row, depth // (n_row * parts)
    f32 = jnp.float32

    def buffer(*shape):
        return pltpu.VMEM(shape + (rank,), f32)

    anywhere = pl.BlockSpec(memory_space=pl.ANY)
    vmem = pl.BlockSpec(memory_space=pltpu.VMEM)
    grad_a, grad_b, grad_c = pl.pallas_call(
        functools.partial(kernel, n_row, n_col, parts),
        out_shape=(
            jax.ShapeDtypeStruct((own_a, rank), f32),
            jax.ShapeDtypeStruct((own_b, rank), f32),
            jax.ShapeDtypeStruct((chips, 2, parts, part_k, rank), f32),
        ),
        in_specs=[anywhere] * 4,
        out_specs=(vmem, vmem, vmem),
        scratch_shapes=[
            pltpu.VMEM(tensor.shape, tensor.dtype),
            buffer(rows_i, rows_j),
            buffer(n_col, own_a),
            buffer(chips, 2, own_b),
            buffer(rows_i),
            buffer(depth),
            pltpu.VMEM((depth, rank), jnp.bfloat16),
            buffer(rank),
            buffer(chips, 2, part_r), buffer(chips, 2, own_b), buffer(chips, 2, parts, part_k),
            buffer(chips, part_r), buffer(chips, own_b), buffer(chips, parts, part_k),
            buffer(chips, part_r), buffer(chips, own_b), buffer(chips, parts, part_k),
            buffer(chips, part_r), buffer(chips, own_b), buffer(chips, n_col, part_k),
            buffer(n_col, own_a),
            buffer(n_col, part_r),
            buffer(n_row, part_r),
            buffer(rows_i),
            buffer(rows_i, 8),
            buffer(chips, 2, 2, part_r),
            buffer(chips, 2, parts, part_k),
            pltpu.SemaphoreType.DMA((rows_i // GROUP,)),
            pltpu.SemaphoreType.DMA((3,)),
            pltpu.SemaphoreType.DMA((4, chips)),
            pltpu.SemaphoreType.DMA((4, chips)),
            pltpu.SemaphoreType.DMA((2, chips, n_col)),
            pltpu.SemaphoreType.DMA((2, chips, n_col)),
            pltpu.SemaphoreType.DMA((BLOCKS + chips,)),
            pltpu.SemaphoreType.DMA((BLOCKS + chips,)),
            pltpu.SemaphoreType.DMA((3, n_col)),
            pltpu.SemaphoreType.DMA((3, n_col)),
        ],
        compiler_params=pltpu.CompilerParams(
            collective_id=0, has_side_effects=True, vmem_limit_bytes=52 * 1024 * 1024
        ),
        cost_estimate=pl.CostEstimate(
            flops=4 * rows_i * rows_j * depth * rank,
            bytes_accessed=2 * rows_i * rows_j * depth,
            transcendentals=0,
        ),
    )(tensor, factor_a, factor_b, factor_c)
    return grad_a, grad_b, grad_c.reshape(depth, rank)


def solution(mesh):
    in_specs = (P("row", "col", None), P(("row", "col"), None), P(("col", "row"), None), P())
    out_specs = (P(("row", "col"), None), P(("col", "row"), None), P())
    body = functools.partial(shards, mesh.shape["row"], mesh.shape["col"])
    return jax.shard_map(body, mesh=mesh, in_specs=in_specs, out_specs=out_specs, check_vma=False)
```

time: 44.6 us -> 41.1 us (0.922)
  Pallas kernels: 39.4 us -> 35.8 us
    pallas_call x1, Pallas kernels: 39.4 us -> 35.8 us  [shards(): pl.pallas_call(functools.partial(kernel, n_row, n_col, parts), out_shape=...]
where the time goes in v2:
time: 41.1 us; the launch traced here: 40.8 us
  Pallas kernels  35.8 us (87%)
  local copies, waits for them, and re-layouts  4.34 us (11%)
  between operations  0.65 us (2%)
    pallas_call x1, Pallas kernels, shards(): pl.pallas_call(functools.partial(kernel, n_row, n_col, parts), out_shape=...  35.8 us
    unnamed x9, local copies, waits for them, and re-layouts  4.34 us

profile of v2, /device:TPU:1, one launch (start us, length us, event | category | flops | bytes accessed | tf_op | source)
XLA Modules:
  0.0 40.8 jit_solution(12354114786408972330)
XLA Ops:
  0.6 0.0 copy-start
  0.6 0.9 %copy-done = f32[256,256]{1,0:T(8,128)S(1)} copy-done((f32[256,256]{1,0:T(8,128)S(1)}, f32[256,256]{1,0:T(8,128)}, u32[]{:S(2)}) %copy-start) | copy-done | bytes 262168
  1.6 0.0 copy-start.1
  1.6 0.8 %copy-done.1 = f32[32,256]{1,0:T(8,128)S(1)} copy-done((f32[32,256]{1,0:T(8,128)S(1)}, f32[32,256]{1,0:T(8,128)}, u32[]{:S(2)}) %copy-start.1) | copy-done | bytes 32792
  2.3 0.0 copy-start.2
  2.3 0.7 %copy-done.2 = f32[16,256]{1,0:T(8,128)S(1)} copy-done((f32[16,256]{1,0:T(8,128)S(1)}, f32[16,256]{1,0:T(8,128)}, u32[]{:S(2)}) %copy-start.2) | copy-done | bytes 16408
  3.1 35.8 %shard_map.67 = (f32[32,256]{1,0:T(8,128)S(1)}, f32[16,256]{1,0:T(8,128)S(1)}, f32[8,2,2,8,256]{4,3,2,1,0:T(8,128)S(1)}) custom-call(bf16[64,256,256]{2,1,0:T(8,128)(2,1)} %t_hbm.1, f32[32,256]{1,0:T(8,128)S(1)} %copy-done.1, f32[16,256]{1,0:T(8,128)S(1)} %copy-done.2, f32[256,256]{1,0:T(8,128)S(1)} %copy-done), custom_call_target="tpu_custom_call" | custom-call | flops 4294967296 | bytes 8388608 | tf_op jit(solution)/shard_map/pallas_call | solution.py:270
  38.9 0.6 %copy.10 = f32[32,256]{1,0:T(8,128)} copy(f32[32,256]{1,0:T(8,128)S(1)} %get-tuple-element.12) | data formatting | bytes 65536
  39.5 0.6 %copy.11 = f32[16,256]{1,0:T(8,128)} copy(f32[16,256]{1,0:T(8,128)S(1)} %get-tuple-element.13) | data formatting | bytes 32768
  40.1 0.7 %copy.12 = f32[256,256]{1,0:T(8,128)} copy(f32[256,256]{1,0:T(8,128)S(1)} %bitcast.1) | data formatting | bytes 524288
Async XLA Ops:
  0.6 1.0 %copy-start = (f32[256,256]{1,0:T(8,128)S(1)}, f32[256,256]{1,0:T(8,128)}, u32[]{:S(2)}) copy-start(f32[256,256]{1,0:T(8,128)} %fc_hbm.1) | copy-start | bytes 786436
  1.6 0.8 %copy-start.1 = (f32[32,256]{1,0:T(8,128)S(1)}, f32[32,256]{1,0:T(8,128)}, u32[]{:S(2)}) copy-start(f32[32,256]{1,0:T(8,128)} %fa_hbm.1) | copy-start | bytes 98308
  2.3 0.7 %copy-start.2 = (f32[16,256]{1,0:T(8,128)S(1)}, f32[16,256]{1,0:T(8,128)}, u32[]{:S(2)}) copy-start(f32[16,256]{1,0:T(8,128)} %fb_hbm.1) | copy-start | bytes 49156
